TPU v7x, 128 devices: a whole 4x4x4 slice. The times are simulated.
128 devices in a mesh: lon: 16 (over x_hi, z, core), lat: 8 (over x_lo, y).
Axes of the slice: x: 4 (x_hi: 2, x_lo: 2; x = x_hi * 2 + x_lo), y: 4, z: 4, core: 2. Of those that a mesh axis runs over, the one named last changes fastest.
Arguments:
- state: bfloat16 [16, 8, 64, 512, 128], P('lon', 'lat'), may hold values from -6 to 6
- conv_w: bfloat16 [3, 8, 16, 16], replicated, may hold values from -0.875 to 0.875
- readout: float32 [128, 8], replicated, may hold values from -0.5 to 0.5
- kernel: float32 [256, 64, 8], replicated, may hold values from -0.25 to 0.25
- cross_col: int32 [16, 8, 8, 256], P('lon', 'lat'), may hold values from 0 to 511
- seg_count: int32 [16, 8, 256], P('lon', 'lat'), may hold values from 1 to 8
- seg_len: float32 [16, 8, 8, 256], P('lon', 'lat'), may hold values from 0.25 to 1
- observed: float32 [16, 8, 256, 256], P('lon', 'lat'), may hold values from -8 to 8
- obs_err: float32 [16, 8, 256, 256], P('lon', 'lat'), may hold values from 0.5 to 2
Outputs:
- grad_state: bfloat16 [16, 8, 64, 512, 128], P('lon', 'lat')
- bending: float32 [16, 8, 256, 256], P('lon', 'lat')
- grad_conv: float32 [3, 8, 16, 16], replicated
Inputs may be any that keep to these rules, and one draw needn't show every extreme that they name: `cross_col`: a column of the crossed tile.
All inputs are finite; a program needn't handle non-finite values.
Results may differ from a plain program's by a relative error of at most 0.0037.
The roundings to bfloat16 on the way count: a program that leaves them out, or rounds other values in their place, can miss the bound.
Values sent between devices are 32-bit elements; how exact they have to be, the bound alone decides.
A program may use at most 192 MiB of HBM per device.

v0:
```python
import jax
import jax.numpy as jnp
from jax import lax
from jax.sharding import PartitionSpec as P


def from_behind(value, axis, steps):
    count = lax.axis_size(axis)
    pairs = [(source, (source + steps) % count) for source in range(count)]
    return lax.ppermute(value, axis, pairs)


def block_weights(conv_w):
    taps, groups, width, _ = conv_w.shape
    eye = jnp.eye(groups, dtype=jnp.float32)
    full = conv_w.astype(jnp.float32)[:, :, :, None, :] * eye[None, :, None, :, None]
    return full.reshape(taps, groups * width, groups * width).astype(jnp.bfloat16)


def on_device(state, conv_w, readout, kernel, cross_col, seg_count, seg_len, observed, obs_err):
    column = state[0, 0]
    levels = column.shape[0]
    ncols = column.shape[1]
    taps = conv_w.shape[0]
    groups = conv_w.shape[1]
    width = conv_w.shape[2]
    wide = block_weights(conv_w)
    padded = jnp.pad(column, ((1, 1), (0, 0), (0, 0)))
    act = jnp.zeros(column.shape, jnp.float32)
    for tap in range(taps):
        act = act + jnp.einsum(
            "lci,ij->lcj", padded[tap : tap + levels], wide[tap], preferred_element_type=jnp.float32
        )
    feat = jax.nn.silu(act)
    profile = jnp.einsum("lcj,jn->cln", feat, readout, precision=lax.Precision.HIGHEST).reshape(
        ncols, -1
    )
    span = cross_col.shape[2]
    rays = cross_col.shape[3]
    lon_n = lax.axis_size("lon")
    here = lax.axis_index("lon")
    every = lax.all_gather(seg_count, "lon", axis=0, tiled=True)[:, 0, :]
    offsets = jnp.arange(span, dtype=jnp.int32)
    owners = (here - offsets) % lon_n
    counts = jnp.take(every, owners, axis=0)
    weight = seg_len[0, 0] * (offsets[:, None] < counts).astype(jnp.float32)
    places = cross_col[0, 0].reshape(-1)
    sampled = jnp.take(profile, places, axis=0).reshape(span, rays, -1) * weight[:, :, None]
    kflat = kernel.reshape(kernel.shape[0], -1)
    carried = sampled[span - 1]
    for step in range(span - 2, -1, -1):
        carried = from_behind(carried, "lon", -1) + sampled[step]
    bending = jnp.einsum("rq,kq->rk", carried, kflat, precision=lax.Precision.HIGHEST)
    adjoint = (bending - observed[0, 0]) / (obs_err[0, 0] * obs_err[0, 0])
    current = jnp.dot(adjoint, kflat, precision=lax.Precision.HIGHEST)
    held = [current]
    for step in range(1, span):
        current = from_behind(current, "lon", 1)
        held.append(current)
    back = jnp.stack(held)
    back = back * weight[:, :, None]
    dprofile = (
        jnp.zeros((ncols, back.shape[2]), jnp.float32)
        .at[places]
        .add(back.reshape(-1, back.shape[2]))
    )
    dfeat = jnp.einsum(
        "cln,jn->lcj", dprofile.reshape(ncols, levels, -1), readout, precision=lax.Precision.HIGHEST
    )
    sig = jax.nn.sigmoid(act)
    dact = (dfeat * sig * (1.0 + act * (1.0 - sig))).astype(jnp.bfloat16)
    dpad = jnp.pad(dact, ((1, 1), (0, 0), (0, 0)))
    grad_x = jnp.zeros(column.shape, jnp.float32)
    grads = []
    for tap in range(taps):
        grad_x = grad_x + jnp.einsum(
            "lcj,ij->lci",
            dpad[2 - tap : 2 - tap + levels],
            wide[tap],
            preferred_element_type=jnp.float32,
        )
        grads.append(
            jnp.einsum(
                "lci,lcj->ij", padded[tap : tap + levels], dact, preferred_element_type=jnp.float32
            )
        )
    grad_w = jnp.stack(grads).reshape(taps, groups, width, groups, width)
    eye = jnp.eye(groups, dtype=jnp.float32)
    grouped = jnp.einsum("tgahb,gh->tgab", grad_w, eye)
    grad_conv = lax.psum(grouped, ("lon", "lat"))
    return (grad_x.astype(jnp.bfloat16)[None, None], bending[None, None], grad_conv)


def solution(mesh):
    in_specs = (
        P("lon", "lat", None, None, None),
        P(),
        P(),
        P(),
        P("lon", "lat", None, None),
        P("lon", "lat", None),
        P("lon", "lat", None, None),
        P("lon", "lat", None, None),
        P("lon", "lat", None, None),
    )
    out_specs = (P("lon", "lat", None, None, None), P("lon", "lat", None, None), P())
    return jax.shard_map(
        on_device, mesh=mesh, in_specs=in_specs, out_specs=out_specs, check_vma=False
    )
```

profile of v0, /device:TPU:1, one launch (start us, length us, event | category | flops | bytes accessed | tf_op | source)
XLA Modules:
  0.0 433.3 jit_solution(11439077147525505158)
XLA Ops:
  0.7 1.1 mul.61
  1.8 0.4 mul.62
  2.5 11.4 %fusion.8 = f32[64,512,128]{2,1,0:T(8,128)} fusion(bf16[1,1,64,512,128]{4,3,2,1,0:T(8,128)(2,1)} %param.9, bf16[3,128,128]{2,1,0:T(8,128)(2,1)S(1)} %multiply_convert_fusion), kind=kOutput, calls=%fused_computation.15 | convolution fusion | flops 1056964608 | bytes 25198592 | tf_op jit(solution)/shard_map/lci,ij->lcj/dot_general | solution.py:31
  14.0 11.4 %fusion.12 = f32[128,64,512]{0,2,1:T(8,128)} fusion(bf16[1,1,64,512,128]{4,3,2,1,0:T(8,128)(2,1)} %param.9, bf16[3,128,128]{2,1,0:T(8,128)(2,1)S(1)} %multiply_convert_fusion), kind=kOutput, calls=%fused_computation.19 | convolution fusion | flops 1073741824 | bytes 25198592 | tf_op jit(solution)/shard_map/lci,ij->lcj/dot_general | solution.py:31
  25.5 21.0 %fusion.2 = f32[64,512,128]{2,1,0:T(8,128)} fusion(f32[64,512,128]{2,1,0:T(8,128)} %fusion.8, f32[128,64,512]{0,2,1:T(8,128)} %fusion.12, bf16[1,1,64,512,128]{4,3,2,1,0:T(8,128)(2,1)} %param.9, bf16[3,128,128]{2,1,0:T(8,128)(2,1)S(1)} %multiply_convert_fusion), kind=kOutput, calls=%fused_computation.7 | convolution fusion | flops 1065353216 | bytes 58753024 | tf_op jit(solution)/shard_map/lci,ij->lcj/dot_general | solution.py:31
  46.5 21.1 %fusion.20 = f32[512,512]{0,1:T(8,128)S(1)} fusion(f32[64,512,128]{2,1,0:T(8,128)} %fusion.2, f32[128,8]{0,1:T(8,128)S(1)} %copy-done.9), kind=kOutput, calls=%fused_computation.30 | convolution fusion | flops 419430400 | bytes 17829888 | tf_op jit(solution)/shard_map/lcj,jn->cln/dot_general | solution.py:35
  68.0 26.7 %all_gather.3 = s32[16,1,256]{2,1,0:T(1,128)S(1)} all-gather(s32[1,1,256]{2,1,0:T(1,128)S(1)} %copy-done.8), channel_id=1, replica_groups=mesh['lon'=16,'lat'=8] {'lon'}, dimensions={0}, use_global_device_ids=true | all-gather | bytes 17408 | tf_op jit(solution)/shard_map/all_gather | solution.py:42
  94.7 8.9 %gather_fusion = f32[2048,512]{1,0:T(8,128)} fusion(f32[512,512]{1,0:T(8,128)S(1)} %copy.40, s32[2048]{0:T(1024)S(1)} %broadcast_clamp_fusion), kind=kCustom, calls=%fused_computation | custom fusion | bytes 8396800 | tf_op jit(solution)/shard_map/jit(_take)/gather | solution.py:48
  103.6 0.6 gather_fusion.1
  104.3 2.7 select_multiply_fusion
  107.2 8.4 %collective-permute-done = f32[256,512]{1,0:T(8,128)S(1)} collective-permute-done((f32[256,512]{1,0:T(8,128)S(1)}, f32[256,512]{1,0:T(8,128)S(1)}, u32[]{:S(2)}, u32[]{:S(2)}) %collective-permute-start) | collective-permute-done | bytes 524320 | tf_op jit(solution)/shard_map/ppermute | solution.py:10
  115.8 8.6 %collective-permute-done.1 = f32[256,512]{1,0:T(8,128)S(1)} collective-permute-done((f32[256,512]{1,0:T(8,128)S(1)}, f32[256,512]{1,0:T(8,128)S(1)}, u32[]{:S(2)}, u32[]{:S(2)}) %collective-permute-start.1) | collective-permute-done | bytes 524320 | tf_op jit(solution)/shard_map/ppermute | solution.py:10
  124.5 2.0 collective-permute-start.2
  126.5 6.7 %collective-permute-done.2 = f32[256,512]{1,0:T(8,128)S(1)} collective-permute-done((f32[256,512]{1,0:T(8,128)S(1)}, f32[256,512]{1,0:T(8,128)S(1)}, u32[]{:S(2)}, u32[]{:S(2)}) %collective-permute-start.2) | collective-permute-done | bytes 524320 | tf_op jit(solution)/shard_map/ppermute | solution.py:10
  133.3 5.6 %collective-permute-start.3 = (f32[256,512]{1,0:T(8,128)S(1)}, f32[256,512]{1,0:T(8,128)S(1)}, u32[]{:S(2)}, u32[]{:S(2)}) collective-permute-start(f32[256,512]{1,0:T(8,128)S(1)} %fusion.39), channel_id=1, source_target_pairs={{0,120},{8,0},{16,8},{24,16},{32,24},{40,32},{48,40},{56,48},{64,5... | collective-permute-start | bytes 1572872 | tf_op jit(solution)/shard_map/ppermute | solution.py:10
  138.9 3.1 collective-permute-done.3
  142.0 9.2 %collective-permute-start.4 = (f32[256,512]{1,0:T(8,128)S(1)}, f32[256,512]{1,0:T(8,128)S(1)}, u32[]{:S(2)}, u32[]{:S(2)}) collective-permute-start(f32[256,512]{1,0:T(8,128)S(1)} %fusion.38), channel_id=1, source_target_pairs={{0,120},{8,0},{16,8},{24,16},{32,24},{40,32},{48,40},{56,48},{64,5... | collective-permute-start | bytes 1572872 | tf_op jit(solution)/shard_map/ppermute | solution.py:10
  151.2 1.5 collective-permute-done.4
  152.9 10.8 %collective-permute-start.5 = (f32[256,512]{1,0:T(8,128)S(1)}, f32[256,512]{1,0:T(8,128)S(1)}, u32[]{:S(2)}, u32[]{:S(2)}) collective-permute-start(f32[256,512]{1,0:T(8,128)S(1)} %fusion.37), channel_id=1, source_target_pairs={{0,120},{8,0},{16,8},{24,16},{32,24},{40,32},{48,40},{56,48},{64,5... | collective-permute-start | bytes 1572872 | tf_op jit(solution)/shard_map/ppermute | solution.py:10
  163.6 1.5 collective-permute-done.5
  165.2 11.0 %collective-permute-start.6 = (f32[256,512]{1,0:T(8,128)S(1)}, f32[256,512]{1,0:T(8,128)S(1)}, u32[]{:S(2)}, u32[]{:S(2)}) collective-permute-start(f32[256,512]{1,0:T(8,128)S(1)} %fusion.36), channel_id=1, source_target_pairs={{0,120},{8,0},{16,8},{24,16},{32,24},{40,32},{48,40},{56,48},{64,5... | collective-permute-start | bytes 1572872 | tf_op jit(solution)/shard_map/ppermute | solution.py:10
  176.2 1.5 collective-permute-done.6
  177.7 0.6 fusion.34
  178.4 1.5 bitcast_dynamic-update-slice_fusion.7
  179.9 12.1 %collective-permute-done.7 = f32[256,512]{1,0:T(8,128)S(1)} collective-permute-done((f32[256,512]{1,0:T(8,128)S(1)}, f32[256,512]{1,0:T(8,128)S(1)}, u32[]{:S(2)}, u32[]{:S(2)}) %collective-permute-start.7) | collective-permute-done | bytes 524320 | tf_op jit(solution)/shard_map/ppermute | solution.py:10
  191.9 12.4 %collective-permute-done.8 = f32[256,512]{1,0:T(8,128)S(1)} collective-permute-done((f32[256,512]{1,0:T(8,128)S(1)}, f32[256,512]{1,0:T(8,128)S(1)}, u32[]{:S(2)}, u32[]{:S(2)}) %collective-permute-start.8) | collective-permute-done | bytes 524320 | tf_op jit(solution)/shard_map/ppermute | solution.py:10
  204.3 12.2 %collective-permute-done.9 = f32[256,512]{1,0:T(8,128)S(1)} collective-permute-done((f32[256,512]{1,0:T(8,128)S(1)}, f32[256,512]{1,0:T(8,128)S(1)}, u32[]{:S(2)}, u32[]{:S(2)}) %collective-permute-start.9) | collective-permute-done | bytes 524320 | tf_op jit(solution)/shard_map/ppermute | solution.py:10
  216.5 12.2 %collective-permute-done.10 = f32[256,512]{1,0:T(8,128)S(1)} collective-permute-done((f32[256,512]{1,0:T(8,128)S(1)}, f32[256,512]{1,0:T(8,128)S(1)}, u32[]{:S(2)}, u32[]{:S(2)}) %collective-permute-start.10) | collective-permute-done | bytes 524320 | tf_op jit(solution)/shard_map/ppermute | solution.py:10
  228.8 12.2 %collective-permute-done.11 = f32[256,512]{1,0:T(8,128)S(1)} collective-permute-done((f32[256,512]{1,0:T(8,128)S(1)}, f32[256,512]{1,0:T(8,128)S(1)}, u32[]{:S(2)}, u32[]{:S(2)}) %collective-permute-start.11) | collective-permute-done | bytes 524320 | tf_op jit(solution)/shard_map/ppermute | solution.py:10
  241.0 0.8 bitcast_dynamic-update-slice_fusion.6
  241.8 0.8 bitcast_dynamic-update-slice_fusion.5
  242.6 0.8 bitcast_dynamic-update-slice_fusion.4
  243.5 9.7 %collective-permute-done.12 = f32[256,512]{1,0:T(8,128)S(1)} collective-permute-done((f32[256,512]{1,0:T(8,128)S(1)}, f32[256,512]{1,0:T(8,128)S(1)}, u32[]{:S(2)}, u32[]{:S(2)}) %collective-permute-start.12) | collective-permute-done | bytes 524320 | tf_op jit(solution)/shard_map/ppermute | solution.py:10
  253.2 0.8 bitcast_dynamic-update-slice_fusion.3
  254.0 0.8 bitcast_dynamic-update-slice_fusion.2
  254.9 0.8 bitcast_dynamic-update-slice_fusion.1
  255.7 9.7 %collective-permute-done.13 = f32[256,512]{1,0:T(8,128)S(1)} collective-permute-done((f32[256,512]{1,0:T(8,128)S(1)}, f32[256,512]{1,0:T(8,128)S(1)}, u32[]{:S(2)}, u32[]{:S(2)}) %collective-permute-start.13) | collective-permute-done | bytes 524320 | tf_op jit(solution)/shard_map/ppermute | solution.py:10
  265.4 0.8 bitcast_dynamic-update-slice_fusion
  266.3 4.5 %bitcast_multiply_fusion.1 = f32[2048,512]{1,0:T(8,128)} fusion(f32[8,256,512]{2,1,0:T(8,128)} %bitcast_dynamic-update-slice_fusion, f32[2048]{0:T(1024)S(1)} %broadcast_select_fusion), kind=kLoop, calls=%fused_computation.25 | loop fusion | flops 1048576 | bytes 8396800 | tf_op jit(solution)/shard_map/mul | solution.py:61
  270.7 13.9 %scatter_custom_fusion = f32[512,512]{1,0:T(8,128)S(1)} fusion(s32[2048]{0:T(1024)S(1)} %bitcast.183, f32[2048,512]{1,0:T(8,128)} %bitcast_multiply_fusion.1, f32[]{:T(128)} %constant.51.clone.1), kind=kCustom, calls=%fused_computation.62 | custom fusion | flops 1048576 | bytes 1049088 | tf_op jit(solution)/shard_map/scatter-add | solution.py:65
  285.0 31.4 %fusion.1 = bf16[64,512,128]{2,1,0:T(8,128)(2,1)S(1)} fusion(f32[64,512,128]{2,1,0:T(8,128)} %fusion.2, f32[512,512]{0,1:T(8,128)S(1)} %copy.41, f32[128,8]{0,1:T(8,128)S(1)} %copy-done.9), kind=kOutput, calls=%fused_computation.5 | convolution fusion | flops 440401920 | bytes 26218496 | tf_op jit(solution)/shard_map/cln,jn->lcj/dot_general | solution.py:67
  316.4 7.4 %fusion.48 = f32[64,512,128]{2,1,0:T(8,128)} fusion(bf16[64,512,128]{2,1,0:T(8,128)(2,1)S(1)} %fusion.1, bf16[3,128,128]{2,1,0:T(8,128)(2,1)S(1)} %multiply_convert_fusion), kind=kOutput, calls=%fused_computation.73 | convolution fusion | flops 1056964608 | bytes 25198592 | tf_op jit(solution)/shard_map/lcj,ij->lci/dot_general | solution.py:76
  323.9 8.3 %fusion.49 = f32[64,512,128]{2,1,0:T(8,128)} fusion(bf16[64,512,128]{2,1,0:T(8,128)(2,1)S(1)} %fusion.1, bf16[3,128,128]{2,1,0:T(8,128)(2,1)S(1)} %multiply_convert_fusion), kind=kOutput, calls=%fused_computation.74 | convolution fusion | flops 1073741824 | bytes 25198592 | tf_op jit(solution)/shard_map/lcj,ij->lci/dot_general | solution.py:76
  332.2 2.4 fusion.23
  334.6 2.4 fusion.26
  337.0 2.4 fusion.29
  340.6 74.6 %psum.7 = f32[3,8,16,16]{3,2,1,0:T(8,128)} all-reduce(f32[3,8,16,16]{3,2,1,0:T(8,128)S(1)} %bitcast.179), channel_id=1, replica_groups=mesh['lon'=16,'lat'=8] {'lon','lat'}, use_global_device_ids=true, to_apply=%region_1.2 | all-reduce | flops 6144 | bytes 49152 | tf_op jit(solution)/shard_map/psum | solution.py:90
  415.3 17.8 %fusion.17 = bf16[1,1,64,512,128]{4,3,2,1,0:T(8,128)(2,1)} fusion(bf16[64,512,128]{2,1,0:T(8,128)(2,1)} %copy-done.2, f32[64,512,128]{2,1,0:T(8,128)} %fusion.48, f32[64,512,128]{2,1,0:T(8,128)} %fusion.49, bf16[3,128,128]{2,1,0:T(8,128)(2,1)S(1)} %multiply_convert_fusion), kind=kOutput, calls=%fused_computation.24 | convolution fusion | flops 1069547520 | bytes 50364416 | tf_op jit(solution)/shard_map/lcj,ij->lci/dot_general | solution.py:76
  (66 shorter events, 3.4 us)
Async XLA Ops:
  0.6 177.1 %copy-start = (f32[256,64,8]{0,2,1:T(8,128)S(1)}, f32[256,64,8]{0,2,1:T(8,128)}, u32[]{:S(2)}) copy-start(f32[256,64,8]{0,2,1:T(8,128)} %param.12) | copy-start | bytes 1572868
  14.0 11.5 %copy-start.6 = (s32[1,1,8,256]{3,2,1,0:T(8,128)S(1)}, s32[1,1,8,256]{3,2,1,0:T(8,128)}, u32[]{:S(2)}) copy-start(s32[1,1,8,256]{3,2,1,0:T(8,128)} %param.13) | copy-start | bytes 24580
  25.5 21.0 %copy-start.9 = (f32[128,8]{0,1:T(8,128)S(1)}, f32[128,8]{0,1:T(8,128)}, u32[]{:S(2)}) copy-start(f32[128,8]{0,1:T(8,128)} %param.11) | copy-start | bytes 12292
  46.5 21.5 %copy-start.8 = (s32[1,1,256]{2,1,0:T(1,128)S(1)}, s32[1,1,256]{2,1,0:T(1,128)}, u32[]{:S(2)}) copy-start(s32[1,1,256]{2,1,0:T(1,128)} %param.14) | copy-start | bytes 3076
  94.7 9.5 %copy-start.7 = (f32[1,1,8,256]{3,2,1,0:T(8,128)S(1)}, f32[1,1,8,256]{3,2,1,0:T(8,128)}, u32[]{:S(2)}) copy-start(f32[1,1,8,256]{3,2,1,0:T(8,128)} %param.15) | copy-start | bytes 24580
  104.3 74.1 %copy-start.4 = (f32[1,1,256,256]{3,2,1,0:T(8,128)S(1)}, f32[1,1,256,256]{3,2,1,0:T(8,128)}, u32[]{:S(2)}) copy-start(f32[1,1,256,256]{3,2,1,0:T(8,128)} %param.16) | copy-start | bytes 786436
  104.3 74.1 %copy-start.5 = (f32[1,1,256,256]{3,2,1,0:T(8,128)S(1)}, f32[1,1,256,256]{3,2,1,0:T(8,128)}, u32[]{:S(2)}) copy-start(f32[1,1,256,256]{3,2,1,0:T(8,128)} %param.17) | copy-start | bytes 786436
  107.0 8.7 %collective-permute-start = (f32[256,512]{1,0:T(8,128)S(1)}, f32[256,512]{1,0:T(8,128)S(1)}, u32[]{:S(2)}, u32[]{:S(2)}) collective-permute-start(f32[256,512]{1,0:T(8,128)S(1)} %slice_bitcast_fusion.7), channel_id=1, source_target_pairs={{0,120},{8,0},{16,8},{24,16},{32,24},{40,32},{48,40},{56,48},{64,5... | collective-permute-start | bytes 1572872 | tf_op jit(solution)/shard_map/ppermute | solution.py:10
  115.8 8.7 %collective-permute-start.1 = (f32[256,512]{1,0:T(8,128)S(1)}, f32[256,512]{1,0:T(8,128)S(1)}, u32[]{:S(2)}, u32[]{:S(2)}) collective-permute-start(f32[256,512]{1,0:T(8,128)S(1)} %fusion.41), channel_id=1, source_target_pairs={{0,120},{8,0},{16,8},{24,16},{32,24},{40,32},{48,40},{56,48},{64,5... | collective-permute-start | bytes 1572872 | tf_op jit(solution)/shard_map/ppermute | solution.py:10
  124.5 8.7 %collective-permute-start.2 = (f32[256,512]{1,0:T(8,128)S(1)}, f32[256,512]{1,0:T(8,128)S(1)}, u32[]{:S(2)}, u32[]{:S(2)}) collective-permute-start(f32[256,512]{1,0:T(8,128)S(1)} %fusion.40), channel_id=1, source_target_pairs={{0,120},{8,0},{16,8},{24,16},{32,24},{40,32},{48,40},{56,48},{64,5... | collective-permute-start | bytes 1572872 | tf_op jit(solution)/shard_map/ppermute | solution.py:10
  133.3 8.7 %collective-permute-start.3 = (f32[256,512]{1,0:T(8,128)S(1)}, f32[256,512]{1,0:T(8,128)S(1)}, u32[]{:S(2)}, u32[]{:S(2)}) collective-permute-start(f32[256,512]{1,0:T(8,128)S(1)} %fusion.39), channel_id=1, source_target_pairs={{0,120},{8,0},{16,8},{24,16},{32,24},{40,32},{48,40},{56,48},{64,5... | collective-permute-start | bytes 1572872 | tf_op jit(solution)/shard_map/ppermute | solution.py:10
  142.0 10.7 %collective-permute-start.4 = (f32[256,512]{1,0:T(8,128)S(1)}, f32[256,512]{1,0:T(8,128)S(1)}, u32[]{:S(2)}, u32[]{:S(2)}) collective-permute-start(f32[256,512]{1,0:T(8,128)S(1)} %fusion.38), channel_id=1, source_target_pairs={{0,120},{8,0},{16,8},{24,16},{32,24},{40,32},{48,40},{56,48},{64,5... | collective-permute-start | bytes 1572872 | tf_op jit(solution)/shard_map/ppermute | solution.py:10
  152.9 12.3 %collective-permute-start.5 = (f32[256,512]{1,0:T(8,128)S(1)}, f32[256,512]{1,0:T(8,128)S(1)}, u32[]{:S(2)}, u32[]{:S(2)}) collective-permute-start(f32[256,512]{1,0:T(8,128)S(1)} %fusion.37), channel_id=1, source_target_pairs={{0,120},{8,0},{16,8},{24,16},{32,24},{40,32},{48,40},{56,48},{64,5... | collective-permute-start | bytes 1572872 | tf_op jit(solution)/shard_map/ppermute | solution.py:10
  165.2 12.5 %collective-permute-start.6 = (f32[256,512]{1,0:T(8,128)S(1)}, f32[256,512]{1,0:T(8,128)S(1)}, u32[]{:S(2)}, u32[]{:S(2)}) collective-permute-start(f32[256,512]{1,0:T(8,128)S(1)} %fusion.36), channel_id=1, source_target_pairs={{0,120},{8,0},{16,8},{24,16},{32,24},{40,32},{48,40},{56,48},{64,5... | collective-permute-start | bytes 1572872 | tf_op jit(solution)/shard_map/ppermute | solution.py:10
  178.4 92.4 %copy-start.3 = (f32[256,256]{1,0:T(8,128)}, f32[256,256]{1,0:T(8,128)S(1)}, u32[]{:S(2)}) copy-start(f32[256,256]{1,0:T(8,128)S(1)} %fusion.34) | copy-start | bytes 786436
  179.9 12.1 %collective-permute-start.7 = (f32[256,512]{1,0:T(8,128)S(1)}, f32[256,512]{1,0:T(8,128)S(1)}, u32[]{:S(2)}, u32[]{:S(2)}) collective-permute-start(f32[256,512]{1,0:T(8,128)S(1)} %get-tuple-element.6), channel_id=1, source_target_pairs={{0,8},{8,16},{16,24},{24,32},{32,40},{40,48},{48,56},{56,64},{64,7... | collective-permute-start | bytes 1572872 | tf_op jit(solution)/shard_map/ppermute | solution.py:10
  191.9 12.4 %collective-permute-start.8 = (f32[256,512]{1,0:T(8,128)S(1)}, f32[256,512]{1,0:T(8,128)S(1)}, u32[]{:S(2)}, u32[]{:S(2)}) collective-permute-start(f32[256,512]{1,0:T(8,128)S(1)} %collective-permute-done.7), channel_id=1, source_target_pairs={{0,8},{8,16},{16,24},{24,32},{32,40},{40,48},{48,56},{56,64},{64,7... | collective-permute-start | bytes 1572872 | tf_op jit(solution)/shard_map/ppermute | solution.py:10
  204.3 12.2 %collective-permute-start.9 = (f32[256,512]{1,0:T(8,128)S(1)}, f32[256,512]{1,0:T(8,128)S(1)}, u32[]{:S(2)}, u32[]{:S(2)}) collective-permute-start(f32[256,512]{1,0:T(8,128)S(1)} %collective-permute-done.8), channel_id=1, source_target_pairs={{0,8},{8,16},{16,24},{24,32},{32,40},{40,48},{48,56},{56,64},{64,7... | collective-permute-start | bytes 1572872 | tf_op jit(solution)/shard_map/ppermute | solution.py:10
  216.5 12.2 %collective-permute-start.10 = (f32[256,512]{1,0:T(8,128)S(1)}, f32[256,512]{1,0:T(8,128)S(1)}, u32[]{:S(2)}, u32[]{:S(2)}) collective-permute-start(f32[256,512]{1,0:T(8,128)S(1)} %collective-permute-done.9), channel_id=1, source_target_pairs={{0,8},{8,16},{16,24},{24,32},{32,40},{40,48},{48,56},{56,64},{64,7... | collective-permute-start | bytes 1572872 | tf_op jit(solution)/shard_map/ppermute | solution.py:10
  228.8 12.2 %collective-permute-start.11 = (f32[256,512]{1,0:T(8,128)S(1)}, f32[256,512]{1,0:T(8,128)S(1)}, u32[]{:S(2)}, u32[]{:S(2)}) collective-permute-start(f32[256,512]{1,0:T(8,128)S(1)} %collective-permute-done.10), channel_id=1, source_target_pairs={{0,8},{8,16},{16,24},{24,32},{32,40},{40,48},{48,56},{56,64},{64,7... | collective-permute-start | bytes 1572872 | tf_op jit(solution)/shard_map/ppermute | solution.py:10
  241.0 12.2 %collective-permute-start.12 = (f32[256,512]{1,0:T(8,128)S(1)}, f32[256,512]{1,0:T(8,128)S(1)}, u32[]{:S(2)}, u32[]{:S(2)}) collective-permute-start(f32[256,512]{1,0:T(8,128)S(1)} %collective-permute-done.11), channel_id=1, source_target_pairs={{0,8},{8,16},{16,24},{24,32},{32,40},{40,48},{48,56},{56,64},{64,7... | collective-permute-start | bytes 1572872 | tf_op jit(solution)/shard_map/ppermute | solution.py:10
  253.2 12.2 %collective-permute-start.13 = (f32[256,512]{1,0:T(8,128)S(1)}, f32[256,512]{1,0:T(8,128)S(1)}, u32[]{:S(2)}, u32[]{:S(2)}) collective-permute-start(f32[256,512]{1,0:T(8,128)S(1)} %collective-permute-done.12), channel_id=1, source_target_pairs={{0,8},{8,16},{16,24},{24,32},{32,40},{40,48},{48,56},{56,64},{64,7... | collective-permute-start | bytes 1572872 | tf_op jit(solution)/shard_map/ppermute | solution.py:10
  316.4 20.5 %copy-start.2 = (bf16[64,512,128]{2,1,0:T(8,128)(2,1)}, bf16[64,512,128]{2,1,0:T(8,128)(2,1)S(1)}, u32[]{:S(2)}) copy-start(bf16[64,512,128]{2,1,0:T(8,128)(2,1)S(1)} %fusion.1) | copy-start | bytes 25165828
  316.4 15.7 %slice-start = ((s8[8388608]{0:T(1024)(128)(4,1)}), s8[4194304]{0:T(1024)(128)(4,1)S(1)}, s32[]{:S(2)}) async-start(s8[8388608]{0:T(1024)(128)(4,1)} %bitcast.175), calls=%async_computation | async-start | bytes 8388608
  323.9 8.3 %slice-start.1 = ((s8[8388608]{0:T(1024)(128)(4,1)}), s8[4194304]{0:T(1024)(128)(4,1)S(1)}, s32[]{:S(2)}) async-start(s8[8388608]{0:T(1024)(128)(4,1)} %bitcast.175), calls=%async_computation.1 | async-start | bytes 8388608
  415.3 17.8 %copy-start.1 = (f32[256,64,8]{0,2,1:T(8,128)S(1)}, f32[256,64,8]{0,2,1:T(8,128)}, u32[]{:S(2)}) copy-start(f32[256,64,8]{0,2,1:T(8,128)} %param.12) | copy-start | bytes 1572868
where the time goes:
time: 440 us; the launch traced here: 433 us
  matrix products  139 us (32%)
  waiting for transfers between devices  112 us (25%)
  blocking collectives  101 us (23%)
  starting transfers between devices  38.8 us (9%)
  other arithmetic  21.7 us (5%)
  local copies, waits for them, and re-layouts  18.8 us (4%)
    ppermute x14, waiting for transfers between devices, from_behind(): return lax.ppermute(value, axis, pairs)  112 us
    psum x1, blocking collectives, on_device(): grad_conv = lax.psum(grouped, ('lon', 'lat'))  74.6 us
    dot_general x3, matrix products, on_device(): jnp.einsum('lci,ij->lcj', padded[tap:tap + levels], wide[tap], preferred_...  43.8 us
    ppermute x14, starting transfers between devices, from_behind(): return lax.ppermute(value, axis, pairs)  38.8 us
    dot_general x3, matrix products, on_device(): jnp.einsum('lcj,ij->lci', dpad[2 - tap:2 - tap + levels], wide[tap], pref...  33.5 us
    dot_general x1, matrix products, on_device(): jnp.einsum('cln,jn->lcj', dprofile.reshape(ncols, levels, -1), readout, p...  31.4 us
    all_gather x1, blocking collectives, on_device(): every = lax.all_gather(seg_count, 'lon', axis=0, tiled=True)[:, 0, :]  26.7 us
    dot_general x1, matrix products, on_device(): jnp.einsum('lcj,jn->cln', feat, readout, precision=lax.Precision.HIGHEST)  21.1 us
  transfers between devices with their start and end apart: 14, of which 14 were waited for; matrix products, arithmetic and copies ran while one was open for 1% of the time, Pallas kernels for 0%

commit v1 on v0

--- a/solution.py
+++ b/solution.py
@@ -39,7 +39,9 @@
     rays = cross_col.shape[3]
     lon_n = lax.axis_size("lon")
     here = lax.axis_index("lon")
-    every = lax.all_gather(seg_count, "lon", axis=0, tiled=True)[:, 0, :]
+    every = jnp.concatenate(
+        lax.all_to_all(jnp.stack([seg_count] * lax.axis_size("lon")), "lon", 0, 0), axis=0
+    )[:, 0, :]
     offsets = jnp.arange(span, dtype=jnp.int32)
     owners = (here - offsets) % lon_n
     counts = jnp.take(every, owners, axis=0)

time: 440 us -> 429 us (0.975)
  blocking collectives: 101 us -> 74.5 us
  starting transfers between devices: 38.8 us -> 63.4 us
  waiting for transfers between devices: 112 us -> 102 us
    all_gather x1 -> x0, blocking collectives: 26.7 us -> none  [on_device(): every = lax.all_gather(seg_count, 'lon', axis=0, tiled=True)[:, 0, :]]
    ppermute x14, starting transfers between devices: 38.8 us -> 54.1 us  [from_behind(): return lax.ppermute(value, axis, pairs)]
    ppermute x14, waiting for transfers between devices: 112 us -> 102 us  [from_behind(): return lax.ppermute(value, axis, pairs)]
    all_to_all x0 -> x1, starting transfers between devices: none -> 9.29 us  [on_device(): lax.all_to_all(jnp.stack([seg_count] * lax.axis_size('lon')), 'lon', 0, 0)]
  transfers between devices with their start and end apart: 14 -> 15, of which waited for: 14 -> 14; matrix products, arithmetic and copies ran while one was open for 1% -> 19% of each run, Pallas kernels for 0% -> 0%
where the time goes in v1:
time: 429 us; the launch traced here: 422 us
  matrix products  139 us (32%)
  waiting for transfers between devices  102 us (24%)
  blocking collectives  74.5 us (17%)
  starting transfers between devices  63.4 us (15%)
  other arithmetic  21.7 us (5%)
  local copies, waits for them, and re-layouts  20.1 us (5%)
    ppermute x14, waiting for transfers between devices, from_behind(): return lax.ppermute(value, axis, pairs)  102 us
    psum x1, blocking collectives, on_device(): grad_conv = lax.psum(grouped, ('lon', 'lat'))  74.5 us
    ppermute x14, starting transfers between devices, from_behind(): return lax.ppermute(value, axis, pairs)  54.1 us
    dot_general x3, matrix products, on_device(): jnp.einsum('lci,ij->lcj', padded[tap:tap + levels], wide[tap], preferred_...  43.8 us
    dot_general x3, matrix products, on_device(): jnp.einsum('lcj,ij->lci', dpad[2 - tap:2 - tap + levels], wide[tap], pref...  33.5 us
    dot_general x1, matrix products, on_device(): jnp.einsum('cln,jn->lcj', dprofile.reshape(ncols, levels, -1), readout, p...  31.4 us
    dot_general x1, matrix products, on_device(): jnp.einsum('lcj,jn->cln', feat, readout, precision=lax.Precision.HIGHEST)  21.1 us
    scatter-add x1, other arithmetic, on_device(): dprofile = jnp.zeros((ncols, back.shape[2]), jnp.float32).at[places].add(...  13.9 us
  transfers between devices with their start and end apart: 15, of which 14 were waited for; matrix products, arithmetic and copies ran while one was open for 19% of the time, Pallas kernels for 0%

profile of v1, /device:TPU:1, one launch (start us, length us, event | category | flops | bytes accessed | tf_op | source)
XLA Modules:
  0.0 422.1 jit_solution(16871828602457294276)
XLA Ops:
  0.6 1.4 stack.60
  2.0 9.3 %all-to-all-start = ((s32[16,1,1,256]{3,2,1,0:T(1,128)}), s32[16,1,1,256]{3,2,1,0:T(1,128)S(1)}, u32[]{:S(2)}, u32[]{:S(2)}) async-start(s32[16,1,1,256]{3,2,1,0:T(1,128)} %stack.60), calls=%async_computation | async-start | bytes 32768 | tf_op jit(solution)/shard_map/all_to_all | solution.py:43
  11.3 1.1 mul.61
  13.1 11.4 %fusion.8 = f32[64,512,128]{2,1,0:T(8,128)} fusion(bf16[1,1,64,512,128]{4,3,2,1,0:T(8,128)(2,1)} %param.9, bf16[3,128,128]{2,1,0:T(8,128)(2,1)S(1)} %multiply_convert_fusion), kind=kOutput, calls=%fused_computation.15 | convolution fusion | flops 1056964608 | bytes 25198592 | tf_op jit(solution)/shard_map/lci,ij->lcj/dot_general | solution.py:31
  24.5 11.4 %fusion.12 = f32[128,64,512]{0,2,1:T(8,128)} fusion(bf16[1,1,64,512,128]{4,3,2,1,0:T(8,128)(2,1)} %param.9, bf16[3,128,128]{2,1,0:T(8,128)(2,1)S(1)} %multiply_convert_fusion), kind=kOutput, calls=%fused_computation.19 | convolution fusion | flops 1073741824 | bytes 25198592 | tf_op jit(solution)/shard_map/lci,ij->lcj/dot_general | solution.py:31
  36.1 21.0 %fusion.2 = f32[64,512,128]{2,1,0:T(8,128)} fusion(f32[64,512,128]{2,1,0:T(8,128)} %fusion.8, f32[128,64,512]{0,2,1:T(8,128)} %fusion.12, bf16[1,1,64,512,128]{4,3,2,1,0:T(8,128)(2,1)} %param.9, bf16[3,128,128]{2,1,0:T(8,128)(2,1)S(1)} %multiply_convert_fusion), kind=kOutput, calls=%fused_computation.7 | convolution fusion | flops 1065353216 | bytes 58753024 | tf_op jit(solution)/shard_map/lci,ij->lcj/dot_general | solution.py:31
  57.1 21.1 %fusion.20 = f32[512,512]{0,1:T(8,128)S(1)} fusion(f32[64,512,128]{2,1,0:T(8,128)} %fusion.2, f32[128,8]{0,1:T(8,128)S(1)} %copy-done.8), kind=kOutput, calls=%fused_computation.30 | convolution fusion | flops 419430400 | bytes 17829888 | tf_op jit(solution)/shard_map/lcj,jn->cln/dot_general | solution.py:35
  78.5 8.9 %gather_fusion = f32[2048,512]{1,0:T(8,128)} fusion(f32[512,512]{1,0:T(8,128)S(1)} %copy.37, s32[2048]{0:T(1024)S(1)} %broadcast_clamp_fusion), kind=kCustom, calls=%fused_computation | custom fusion | bytes 8396800 | tf_op jit(solution)/shard_map/jit(_take)/gather | solution.py:50
  88.1 2.7 select_multiply_fusion
  91.0 8.5 %collective-permute-done = f32[256,512]{1,0:T(8,128)S(1)} collective-permute-done((f32[256,512]{1,0:T(8,128)S(1)}, f32[256,512]{1,0:T(8,128)S(1)}, u32[]{:S(2)}, u32[]{:S(2)}) %collective-permute-start) | collective-permute-done | bytes 524320 | tf_op jit(solution)/shard_map/ppermute | solution.py:10
  99.6 3.6 collective-permute-start.1
  103.1 5.1 %collective-permute-done.1 = f32[256,512]{1,0:T(8,128)S(1)} collective-permute-done((f32[256,512]{1,0:T(8,128)S(1)}, f32[256,512]{1,0:T(8,128)S(1)}, u32[]{:S(2)}, u32[]{:S(2)}) %collective-permute-start.1) | collective-permute-done | bytes 524320 | tf_op jit(solution)/shard_map/ppermute | solution.py:10
  108.3 7.2 %collective-permute-start.2 = (f32[256,512]{1,0:T(8,128)S(1)}, f32[256,512]{1,0:T(8,128)S(1)}, u32[]{:S(2)}, u32[]{:S(2)}) collective-permute-start(f32[256,512]{1,0:T(8,128)S(1)} %fusion.40), channel_id=1, source_target_pairs={{0,120},{8,0},{16,8},{24,16},{32,24},{40,32},{48,40},{56,48},{64,5... | collective-permute-start | bytes 1572872 | tf_op jit(solution)/shard_map/ppermute | solution.py:10
  115.5 1.5 collective-permute-done.2
  117.1 10.8 %collective-permute-start.3 = (f32[256,512]{1,0:T(8,128)S(1)}, f32[256,512]{1,0:T(8,128)S(1)}, u32[]{:S(2)}, u32[]{:S(2)}) collective-permute-start(f32[256,512]{1,0:T(8,128)S(1)} %fusion.39), channel_id=1, source_target_pairs={{0,120},{8,0},{16,8},{24,16},{32,24},{40,32},{48,40},{56,48},{64,5... | collective-permute-start | bytes 1572872 | tf_op jit(solution)/shard_map/ppermute | solution.py:10
  127.9 1.5 collective-permute-done.3
  129.5 10.8 %collective-permute-start.4 = (f32[256,512]{1,0:T(8,128)S(1)}, f32[256,512]{1,0:T(8,128)S(1)}, u32[]{:S(2)}, u32[]{:S(2)}) collective-permute-start(f32[256,512]{1,0:T(8,128)S(1)} %fusion.38), channel_id=1, source_target_pairs={{0,120},{8,0},{16,8},{24,16},{32,24},{40,32},{48,40},{56,48},{64,5... | collective-permute-start | bytes 1572872 | tf_op jit(solution)/shard_map/ppermute | solution.py:10
  140.2 1.5 collective-permute-done.4
  141.9 10.8 %collective-permute-start.5 = (f32[256,512]{1,0:T(8,128)S(1)}, f32[256,512]{1,0:T(8,128)S(1)}, u32[]{:S(2)}, u32[]{:S(2)}) collective-permute-start(f32[256,512]{1,0:T(8,128)S(1)} %fusion.37), channel_id=1, source_target_pairs={{0,120},{8,0},{16,8},{24,16},{32,24},{40,32},{48,40},{56,48},{64,5... | collective-permute-start | bytes 1572872 | tf_op jit(solution)/shard_map/ppermute | solution.py:10
  152.6 1.5 collective-permute-done.5
  154.2 11.0 %collective-permute-start.6 = (f32[256,512]{1,0:T(8,128)S(1)}, f32[256,512]{1,0:T(8,128)S(1)}, u32[]{:S(2)}, u32[]{:S(2)}) collective-permute-start(f32[256,512]{1,0:T(8,128)S(1)} %fusion.36), channel_id=1, source_target_pairs={{0,120},{8,0},{16,8},{24,16},{32,24},{40,32},{48,40},{56,48},{64,5... | collective-permute-start | bytes 1572872 | tf_op jit(solution)/shard_map/ppermute | solution.py:10
  165.2 1.5 collective-permute-done.6
  166.8 0.6 fusion.34
  167.4 1.5 bitcast_dynamic-update-slice_fusion.7
  168.9 12.1 %collective-permute-done.7 = f32[256,512]{1,0:T(8,128)S(1)} collective-permute-done((f32[256,512]{1,0:T(8,128)S(1)}, f32[256,512]{1,0:T(8,128)S(1)}, u32[]{:S(2)}, u32[]{:S(2)}) %collective-permute-start.7) | collective-permute-done | bytes 524320 | tf_op jit(solution)/shard_map/ppermute | solution.py:10
  181.0 12.4 %collective-permute-done.8 = f32[256,512]{1,0:T(8,128)S(1)} collective-permute-done((f32[256,512]{1,0:T(8,128)S(1)}, f32[256,512]{1,0:T(8,128)S(1)}, u32[]{:S(2)}, u32[]{:S(2)}) %collective-permute-start.8) | collective-permute-done | bytes 524320 | tf_op jit(solution)/shard_map/ppermute | solution.py:10
  193.3 12.2 %collective-permute-done.9 = f32[256,512]{1,0:T(8,128)S(1)} collective-permute-done((f32[256,512]{1,0:T(8,128)S(1)}, f32[256,512]{1,0:T(8,128)S(1)}, u32[]{:S(2)}, u32[]{:S(2)}) %collective-permute-start.9) | collective-permute-done | bytes 524320 | tf_op jit(solution)/shard_map/ppermute | solution.py:10
  205.6 12.2 %collective-permute-done.10 = f32[256,512]{1,0:T(8,128)S(1)} collective-permute-done((f32[256,512]{1,0:T(8,128)S(1)}, f32[256,512]{1,0:T(8,128)S(1)}, u32[]{:S(2)}, u32[]{:S(2)}) %collective-permute-start.10) | collective-permute-done | bytes 524320 | tf_op jit(solution)/shard_map/ppermute | solution.py:10
  217.8 12.2 %collective-permute-done.11 = f32[256,512]{1,0:T(8,128)S(1)} collective-permute-done((f32[256,512]{1,0:T(8,128)S(1)}, f32[256,512]{1,0:T(8,128)S(1)}, u32[]{:S(2)}, u32[]{:S(2)}) %collective-permute-start.11) | collective-permute-done | bytes 524320 | tf_op jit(solution)/shard_map/ppermute | solution.py:10
  230.0 0.8 bitcast_dynamic-update-slice_fusion.6
  230.8 0.8 bitcast_dynamic-update-slice_fusion.5
  231.7 0.8 bitcast_dynamic-update-slice_fusion.4
  232.5 9.7 %collective-permute-done.12 = f32[256,512]{1,0:T(8,128)S(1)} collective-permute-done((f32[256,512]{1,0:T(8,128)S(1)}, f32[256,512]{1,0:T(8,128)S(1)}, u32[]{:S(2)}, u32[]{:S(2)}) %collective-permute-start.12) | collective-permute-done | bytes 524320 | tf_op jit(solution)/shard_map/ppermute | solution.py:10
  242.2 0.8 bitcast_dynamic-update-slice_fusion.3
  243.1 0.8 bitcast_dynamic-update-slice_fusion.2
  243.9 0.8 bitcast_dynamic-update-slice_fusion.1
  244.7 9.7 %collective-permute-done.13 = f32[256,512]{1,0:T(8,128)S(1)} collective-permute-done((f32[256,512]{1,0:T(8,128)S(1)}, f32[256,512]{1,0:T(8,128)S(1)}, u32[]{:S(2)}, u32[]{:S(2)}) %collective-permute-start.13) | collective-permute-done | bytes 524320 | tf_op jit(solution)/shard_map/ppermute | solution.py:10
  254.4 0.8 bitcast_dynamic-update-slice_fusion
  255.3 4.5 %bitcast_multiply_fusion.1 = f32[2048,512]{1,0:T(8,128)} fusion(f32[8,256,512]{2,1,0:T(8,128)} %bitcast_dynamic-update-slice_fusion, f32[2048]{0:T(1024)S(1)} %broadcast_select_fusion), kind=kLoop, calls=%fused_computation.25 | loop fusion | flops 1048576 | bytes 8396800 | tf_op jit(solution)/shard_map/mul | solution.py:63
  259.7 13.9 %scatter_custom_fusion = f32[512,512]{1,0:T(8,128)S(1)} fusion(s32[2048]{0:T(1024)S(1)} %bitcast.184, f32[2048,512]{1,0:T(8,128)} %bitcast_multiply_fusion.1, f32[]{:T(128)} %constant.51.clone.1), kind=kCustom, calls=%fused_computation.62 | custom fusion | flops 1048576 | bytes 1049088 | tf_op jit(solution)/shard_map/scatter-add | solution.py:67
  274.0 31.4 %fusion.1 = bf16[64,512,128]{2,1,0:T(8,128)(2,1)S(1)} fusion(f32[64,512,128]{2,1,0:T(8,128)} %fusion.2, f32[512,512]{0,1:T(8,128)S(1)} %copy.38, f32[128,8]{0,1:T(8,128)S(1)} %copy-done.8), kind=kOutput, calls=%fused_computation.5 | convolution fusion | flops 440401920 | bytes 26218496 | tf_op jit(solution)/shard_map/cln,jn->lcj/dot_general | solution.py:69
  305.5 7.4 %fusion.48 = f32[64,512,128]{2,1,0:T(8,128)} fusion(bf16[64,512,128]{2,1,0:T(8,128)(2,1)S(1)} %fusion.1, bf16[3,128,128]{2,1,0:T(8,128)(2,1)S(1)} %multiply_convert_fusion), kind=kOutput, calls=%fused_computation.73 | convolution fusion | flops 1056964608 | bytes 25198592 | tf_op jit(solution)/shard_map/lcj,ij->lci/dot_general | solution.py:78
  312.9 8.3 %fusion.49 = f32[64,512,128]{2,1,0:T(8,128)} fusion(bf16[64,512,128]{2,1,0:T(8,128)(2,1)S(1)} %fusion.1, bf16[3,128,128]{2,1,0:T(8,128)(2,1)S(1)} %multiply_convert_fusion), kind=kOutput, calls=%fused_computation.74 | convolution fusion | flops 1073741824 | bytes 25198592 | tf_op jit(solution)/shard_map/lcj,ij->lci/dot_general | solution.py:78
  321.2 2.4 fusion.23
  323.6 2.4 fusion.26
  326.0 2.4 fusion.29
  329.6 74.5 %psum.7 = f32[3,8,16,16]{3,2,1,0:T(8,128)} all-reduce(f32[3,8,16,16]{3,2,1,0:T(8,128)S(1)} %bitcast.180), channel_id=1, replica_groups=mesh['lon'=16,'lat'=8] {'lon','lat'}, use_global_device_ids=true, to_apply=%region_1.2 | all-reduce | flops 6144 | bytes 49152 | tf_op jit(solution)/shard_map/psum | solution.py:92
  404.1 17.8 %fusion.17 = bf16[1,1,64,512,128]{4,3,2,1,0:T(8,128)(2,1)} fusion(bf16[64,512,128]{2,1,0:T(8,128)(2,1)} %copy-done.2, f32[64,512,128]{2,1,0:T(8,128)} %fusion.48, f32[64,512,128]{2,1,0:T(8,128)} %fusion.49, bf16[3,128,128]{2,1,0:T(8,128)(2,1)S(1)} %multiply_convert_fusion), kind=kOutput, calls=%fused_computation.24 | convolution fusion | flops 1069547520 | bytes 50364416 | tf_op jit(solution)/shard_map/lcj,ij->lci/dot_general | solution.py:78
  (66 shorter events, 4.2 us)
Async XLA Ops:
  0.6 166.1 %copy-start = (f32[256,64,8]{0,2,1:T(8,128)S(1)}, f32[256,64,8]{0,2,1:T(8,128)}, u32[]{:S(2)}) copy-start(f32[256,64,8]{0,2,1:T(8,128)} %param.12) | copy-start | bytes 1572868
  2.0 85.4 %all-to-all-start = ((s32[16,1,1,256]{3,2,1,0:T(1,128)}), s32[16,1,1,256]{3,2,1,0:T(1,128)S(1)}, u32[]{:S(2)}, u32[]{:S(2)}) async-start(s32[16,1,1,256]{3,2,1,0:T(1,128)} %stack.60), calls=%async_computation | async-start | bytes 32768 | tf_op jit(solution)/shard_map/all_to_all | solution.py:43
  24.5 11.4 %copy-start.6 = (s32[1,1,8,256]{3,2,1,0:T(8,128)S(1)}, s32[1,1,8,256]{3,2,1,0:T(8,128)}, u32[]{:S(2)}) copy-start(s32[1,1,8,256]{3,2,1,0:T(8,128)} %param.13) | copy-start | bytes 24580
  36.1 21.0 %copy-start.8 = (f32[128,8]{0,1:T(8,128)S(1)}, f32[128,8]{0,1:T(8,128)}, u32[]{:S(2)}) copy-start(f32[128,8]{0,1:T(8,128)} %param.11) | copy-start | bytes 12292
  78.5 9.5 %copy-start.7 = (f32[1,1,8,256]{3,2,1,0:T(8,128)S(1)}, f32[1,1,8,256]{3,2,1,0:T(8,128)}, u32[]{:S(2)}) copy-start(f32[1,1,8,256]{3,2,1,0:T(8,128)} %param.15) | copy-start | bytes 24580
  88.1 79.3 %copy-start.4 = (f32[1,1,256,256]{3,2,1,0:T(8,128)S(1)}, f32[1,1,256,256]{3,2,1,0:T(8,128)}, u32[]{:S(2)}) copy-start(f32[1,1,256,256]{3,2,1,0:T(8,128)} %param.16) | copy-start | bytes 786436
  88.1 79.3 %copy-start.5 = (f32[1,1,256,256]{3,2,1,0:T(8,128)S(1)}, f32[1,1,256,256]{3,2,1,0:T(8,128)}, u32[]{:S(2)}) copy-start(f32[1,1,256,256]{3,2,1,0:T(8,128)} %param.17) | copy-start | bytes 786436
  90.8 8.7 %collective-permute-start = (f32[256,512]{1,0:T(8,128)S(1)}, f32[256,512]{1,0:T(8,128)S(1)}, u32[]{:S(2)}, u32[]{:S(2)}) collective-permute-start(f32[256,512]{1,0:T(8,128)S(1)} %slice_bitcast_fusion.7), channel_id=1, source_target_pairs={{0,120},{8,0},{16,8},{24,16},{32,24},{40,32},{48,40},{56,48},{64,5... | collective-permute-start | bytes 1572872 | tf_op jit(solution)/shard_map/ppermute | solution.py:10
  99.6 8.7 %collective-permute-start.1 = (f32[256,512]{1,0:T(8,128)S(1)}, f32[256,512]{1,0:T(8,128)S(1)}, u32[]{:S(2)}, u32[]{:S(2)}) collective-permute-start(f32[256,512]{1,0:T(8,128)S(1)} %fusion.41), channel_id=1, source_target_pairs={{0,120},{8,0},{16,8},{24,16},{32,24},{40,32},{48,40},{56,48},{64,5... | collective-permute-start | bytes 1572872 | tf_op jit(solution)/shard_map/ppermute | solution.py:10
  108.3 8.7 %collective-permute-start.2 = (f32[256,512]{1,0:T(8,128)S(1)}, f32[256,512]{1,0:T(8,128)S(1)}, u32[]{:S(2)}, u32[]{:S(2)}) collective-permute-start(f32[256,512]{1,0:T(8,128)S(1)} %fusion.40), channel_id=1, source_target_pairs={{0,120},{8,0},{16,8},{24,16},{32,24},{40,32},{48,40},{56,48},{64,5... | collective-permute-start | bytes 1572872 | tf_op jit(solution)/shard_map/ppermute | solution.py:10
  117.1 12.3 %collective-permute-start.3 = (f32[256,512]{1,0:T(8,128)S(1)}, f32[256,512]{1,0:T(8,128)S(1)}, u32[]{:S(2)}, u32[]{:S(2)}) collective-permute-start(f32[256,512]{1,0:T(8,128)S(1)} %fusion.39), channel_id=1, source_target_pairs={{0,120},{8,0},{16,8},{24,16},{32,24},{40,32},{48,40},{56,48},{64,5... | collective-permute-start | bytes 1572872 | tf_op jit(solution)/shard_map/ppermute | solution.py:10
  129.5 12.3 %collective-permute-start.4 = (f32[256,512]{1,0:T(8,128)S(1)}, f32[256,512]{1,0:T(8,128)S(1)}, u32[]{:S(2)}, u32[]{:S(2)}) collective-permute-start(f32[256,512]{1,0:T(8,128)S(1)} %fusion.38), channel_id=1, source_target_pairs={{0,120},{8,0},{16,8},{24,16},{32,24},{40,32},{48,40},{56,48},{64,5... | collective-permute-start | bytes 1572872 | tf_op jit(solution)/shard_map/ppermute | solution.py:10
  141.9 12.3 %collective-permute-start.5 = (f32[256,512]{1,0:T(8,128)S(1)}, f32[256,512]{1,0:T(8,128)S(1)}, u32[]{:S(2)}, u32[]{:S(2)}) collective-permute-start(f32[256,512]{1,0:T(8,128)S(1)} %fusion.37), channel_id=1, source_target_pairs={{0,120},{8,0},{16,8},{24,16},{32,24},{40,32},{48,40},{56,48},{64,5... | collective-permute-start | bytes 1572872 | tf_op jit(solution)/shard_map/ppermute | solution.py:10
  154.2 12.5 %collective-permute-start.6 = (f32[256,512]{1,0:T(8,128)S(1)}, f32[256,512]{1,0:T(8,128)S(1)}, u32[]{:S(2)}, u32[]{:S(2)}) collective-permute-start(f32[256,512]{1,0:T(8,128)S(1)} %fusion.36), channel_id=1, source_target_pairs={{0,120},{8,0},{16,8},{24,16},{32,24},{40,32},{48,40},{56,48},{64,5... | collective-permute-start | bytes 1572872 | tf_op jit(solution)/shard_map/ppermute | solution.py:10
  167.4 92.4 %copy-start.3 = (f32[256,256]{1,0:T(8,128)}, f32[256,256]{1,0:T(8,128)S(1)}, u32[]{:S(2)}) copy-start(f32[256,256]{1,0:T(8,128)S(1)} %fusion.34) | copy-start | bytes 786436
  168.9 12.1 %collective-permute-start.7 = (f32[256,512]{1,0:T(8,128)S(1)}, f32[256,512]{1,0:T(8,128)S(1)}, u32[]{:S(2)}, u32[]{:S(2)}) collective-permute-start(f32[256,512]{1,0:T(8,128)S(1)} %get-tuple-element.6), channel_id=1, source_target_pairs={{0,8},{8,16},{16,24},{24,32},{32,40},{40,48},{48,56},{56,64},{64,7... | collective-permute-start | bytes 1572872 | tf_op jit(solution)/shard_map/ppermute | solution.py:10
  181.0 12.4 %collective-permute-start.8 = (f32[256,512]{1,0:T(8,128)S(1)}, f32[256,512]{1,0:T(8,128)S(1)}, u32[]{:S(2)}, u32[]{:S(2)}) collective-permute-start(f32[256,512]{1,0:T(8,128)S(1)} %collective-permute-done.7), channel_id=1, source_target_pairs={{0,8},{8,16},{16,24},{24,32},{32,40},{40,48},{48,56},{56,64},{64,7... | collective-permute-start | bytes 1572872 | tf_op jit(solution)/shard_map/ppermute | solution.py:10
  193.3 12.2 %collective-permute-start.9 = (f32[256,512]{1,0:T(8,128)S(1)}, f32[256,512]{1,0:T(8,128)S(1)}, u32[]{:S(2)}, u32[]{:S(2)}) collective-permute-start(f32[256,512]{1,0:T(8,128)S(1)} %collective-permute-done.8), channel_id=1, source_target_pairs={{0,8},{8,16},{16,24},{24,32},{32,40},{40,48},{48,56},{56,64},{64,7... | collective-permute-start | bytes 1572872 | tf_op jit(solution)/shard_map/ppermute | solution.py:10
  205.6 12.2 %collective-permute-start.10 = (f32[256,512]{1,0:T(8,128)S(1)}, f32[256,512]{1,0:T(8,128)S(1)}, u32[]{:S(2)}, u32[]{:S(2)}) collective-permute-start(f32[256,512]{1,0:T(8,128)S(1)} %collective-permute-done.9), channel_id=1, source_target_pairs={{0,8},{8,16},{16,24},{24,32},{32,40},{40,48},{48,56},{56,64},{64,7... | collective-permute-start | bytes 1572872 | tf_op jit(solution)/shard_map/ppermute | solution.py:10
  217.8 12.2 %collective-permute-start.11 = (f32[256,512]{1,0:T(8,128)S(1)}, f32[256,512]{1,0:T(8,128)S(1)}, u32[]{:S(2)}, u32[]{:S(2)}) collective-permute-start(f32[256,512]{1,0:T(8,128)S(1)} %collective-permute-done.10), channel_id=1, source_target_pairs={{0,8},{8,16},{16,24},{24,32},{32,40},{40,48},{48,56},{56,64},{64,7... | collective-permute-start | bytes 1572872 | tf_op jit(solution)/shard_map/ppermute | solution.py:10
  230.0 12.2 %collective-permute-start.12 = (f32[256,512]{1,0:T(8,128)S(1)}, f32[256,512]{1,0:T(8,128)S(1)}, u32[]{:S(2)}, u32[]{:S(2)}) collective-permute-start(f32[256,512]{1,0:T(8,128)S(1)} %collective-permute-done.11), channel_id=1, source_target_pairs={{0,8},{8,16},{16,24},{24,32},{32,40},{40,48},{48,56},{56,64},{64,7... | collective-permute-start | bytes 1572872 | tf_op jit(solution)/shard_map/ppermute | solution.py:10
  242.2 12.2 %collective-permute-start.13 = (f32[256,512]{1,0:T(8,128)S(1)}, f32[256,512]{1,0:T(8,128)S(1)}, u32[]{:S(2)}, u32[]{:S(2)}) collective-permute-start(f32[256,512]{1,0:T(8,128)S(1)} %collective-permute-done.12), channel_id=1, source_target_pairs={{0,8},{8,16},{16,24},{24,32},{32,40},{40,48},{48,56},{56,64},{64,7... | collective-permute-start | bytes 1572872 | tf_op jit(solution)/shard_map/ppermute | solution.py:10
  305.4 20.5 %copy-start.2 = (bf16[64,512,128]{2,1,0:T(8,128)(2,1)}, bf16[64,512,128]{2,1,0:T(8,128)(2,1)S(1)}, u32[]{:S(2)}) copy-start(bf16[64,512,128]{2,1,0:T(8,128)(2,1)S(1)} %fusion.1) | copy-start | bytes 25165828
  305.4 15.7 %slice-start = ((s8[8388608]{0:T(1024)(128)(4,1)}), s8[4194304]{0:T(1024)(128)(4,1)S(1)}, s32[]{:S(2)}) async-start(s8[8388608]{0:T(1024)(128)(4,1)} %bitcast.176), calls=%async_computation.1 | async-start | bytes 8388608
  312.9 8.3 %slice-start.1 = ((s8[8388608]{0:T(1024)(128)(4,1)}), s8[4194304]{0:T(1024)(128)(4,1)S(1)}, s32[]{:S(2)}) async-start(s8[8388608]{0:T(1024)(128)(4,1)} %bitcast.176), calls=%async_computation.2 | async-start | bytes 8388608
  404.1 17.8 %copy-start.1 = (f32[256,64,8]{0,2,1:T(8,128)S(1)}, f32[256,64,8]{0,2,1:T(8,128)}, u32[]{:S(2)}) copy-start(f32[256,64,8]{0,2,1:T(8,128)} %param.12) | copy-start | bytes 1572868
